TPU v7x, 512 devices: a whole 4x8x8 slice. The times are simulated.
512 devices in a mesh: cuts: 8 (over x, core), rows: 64 (over z, y).
Axes of the slice: x: 4, y: 8, z: 8, core: 2. Of those that a mesh axis runs over, the one named last changes fastest.
Arguments:
- start_modes: float32 [8, 256, 512, 128], P('cuts', 'rows'), may hold values from -6 to 6
- contrast: float32 [8, 256, 512], P('cuts', 'rows'), may hold values from 0 to 1
- rotations: float32 [8, 2, 128, 128], P('cuts'), may hold values from -0.2 to 1.2, as said below
- ordering: int32 [8, 2, 128], P('cuts'), may hold values from 0 to 127, each once within a row
Outputs:
- modes: float32 [8, 256, 512, 128], P('cuts', 'rows')
- coupling: float32 [8, 128, 128], P('cuts', 'rows')
- rayleigh: float32 [8, 128, 128], P('cuts', 'rows')
Inputs may be any that keep to these rules, and one draw needn't show every extreme that they name: `rotations`: each matrix is invertible.
All inputs are finite; a program needn't handle non-finite values.
Results may differ from a plain program's by a relative error of at most 0.00026.
Values sent between devices are 32-bit elements; how exact they have to be, the bound alone decides.
A program may use at most 64 MiB of HBM per device.

v0:
```python
import jax
import jax.numpy as jnp
from jax import lax
from jax.sharding import PartitionSpec as P

DEGREE = 4
ITERS = 2


def padded_2(block, sides, width):
    for axis, dim in sides:
        count = lax.axis_size(axis)
        forward = [(i, i + 1) for i in range(count - 1)]
        backward = [(target, source) for source, target in forward]
        low = lax.ppermute(
            lax.slice_in_dim(block, block.shape[dim] - width, None, axis=dim), axis, forward
        )
        high = lax.ppermute(lax.slice_in_dim(block, 0, width, axis=dim), axis, backward)
        block = jnp.concatenate([low, block, high], axis=dim)
    return block


def from_behind(value, axis, by):
    peers = lax.axis_size(axis)
    pairs = [(i, i + by) for i in range(peers) if 0 <= i + by < peers]
    return lax.ppermute(value, axis, pairs)


def neighbour_sum(center, rows_source):
    columns = jnp.pad(center, ((0, 0), (1, 1), (0, 0)))
    return rows_source[2:] + rows_source[:-2] + columns[:, 2:] + columns[:, :-2]


def operator_core(center, rows_source, section):
    return (
        0.8 * (section[:, :, None] * center + 0.25 * neighbour_sum(center, rows_source))
        - 0.2 * center
    )


def inner_modes(left, right):
    return jnp.einsum("rcm,rcn->mn", left, right, precision=lax.Precision.HIGHEST)


def apply_edge(vectors, section):
    padded = padded_2(vectors, (("rows", 0),), 1)
    return operator_core(vectors, padded, section)


def body(start_modes, contrast, rotations, ordering):
    subspace = start_modes[0]
    section = contrast[0]
    turnings = rotations[0]
    sequence = ordering[0]
    rows_here = subspace.shape[0]
    columns = subspace.shape[1]
    nmodes = subspace.shape[2]
    tiles = lax.axis_size("rows")
    pixels = rows_here * tiles * columns
    for sweep in range(ITERS):
        before = subspace
        current = apply_edge(before, section)
        for degree_step in range(2, DEGREE + 1):
            following = 2.0 * apply_edge(current, section) - before
            before, current = (current, following)
        gram_sum = lax.psum(inner_modes(current, current), "rows") / pixels
        factor_low = jnp.linalg.cholesky(gram_sum)
        mixing = lax.linalg.triangular_solve(
            factor_low, turnings[sweep], left_side=True, lower=True, transpose_a=True
        )
        picker = (sequence[sweep][None, :] == jnp.arange(nmodes, dtype=jnp.int32)[:, None]).astype(
            jnp.float32
        )
        mixing = jnp.dot(mixing, picker, precision=lax.Precision.HIGHEST)
        subspace = jnp.einsum("rcm,mn->rcn", current, mixing, precision=lax.Precision.HIGHEST)
    earlier = from_behind(subspace, "cuts", 1)
    earlier = jnp.where(lax.axis_index("cuts") == 0, start_modes[0], earlier)
    applied = apply_edge(subspace, section)
    coupling_term = inner_modes(earlier, subspace)
    rayleigh_term = inner_modes(subspace, applied)
    share_rows = nmodes // tiles
    coupling_sum, rayleigh_sum = lax.psum((coupling_term, rayleigh_term), "rows")
    coupling_part = lax.dynamic_slice_in_dim(
        coupling_sum, lax.axis_index("rows") * share_rows, share_rows, 0
    )
    rayleigh_part = lax.dynamic_slice_in_dim(
        rayleigh_sum, lax.axis_index("rows") * share_rows, share_rows, 0
    )
    return (subspace[None], (coupling_part / pixels)[None], (rayleigh_part / pixels)[None])


def solution(mesh):
    placed = (
        P("cuts", "rows", None, None),
        P("cuts", "rows", None),
        P("cuts", None, None, None),
        P("cuts", None, None),
    )
    return jax.shard_map(
        body,
        mesh=mesh,
        in_specs=placed,
        out_specs=(P("cuts", "rows", None, None), P("cuts", "rows", None), P("cuts", "rows", None)),
        check_vma=False,
    )
```

profile of v0, /device:TPU:2, one launch (start us, length us, event | category | flops | bytes accessed | tf_op | source)
XLA Modules:
  0.0 658.3 jit_solution(1508440093911116403)
XLA Ops:
  9.7 4.6 collective-permute-start.1
  14.2 4.1 collective-permute-done
  22.1 5.0 collective-permute-start.3
  27.1 3.2 collective-permute-done.2
  33.4 5.0 collective-permute-start.5
  38.4 2.4 collective-permute-done.4
  44.8 5.0 collective-permute-start.7
  49.8 2.4 collective-permute-done.6
  54.2 2.5 convolution_bitcast_fusion.5
  57.0 164.5 %all-reduce.14.cloned.1.call-done = f32[128,128]{0,1:T(8,128)} async-done(((f32[128,128]{0,1:T(8,128)}), f32[128,128]{0,1:T(8,128)}) %all-reduce.14.cloned.1.call-update) | async-done | bytes 65552 | tf_op jit(solution)/shard_map/psum | solution.py:66
  223.3 11.7 %cholesky.44 = f32[128,128]{1,0:T(8,128)S(1)} custom-call(f32[128,128]{1,0:T(8,128)S(1)} %fusion.98), custom_call_target="Cholesky" | custom-call | tf_op jit(solution)/shard_map/jit(cholesky)/cholesky | solution.py:67
  236.4 9.8 %custom-call.6 = f32[1,128,128]{1,2,0:T(8,128)S(1)} custom-call(f32[1,128,128]{2,1,0:T(8,128)S(1)} %fusion.89), custom_call_target="InvertDiagBlocksLowerTriangular" | custom-call | tf_op jit(solution)/shard_map/triangular_solve/custom-call.0 | solution.py:68
  248.9 4.6 collective-permute-start.9
  253.5 2.4 collective-permute-done.8
  259.2 5.0 collective-permute-start.11
  264.3 2.4 collective-permute-done.10
  266.6 1.7 collective-permute-done.11
  270.3 5.0 collective-permute-start.13
  275.3 2.8 collective-permute-done.12
  278.1 1.7 collective-permute-done.13
  282.4 5.3 collective-permute-start.15
  287.8 2.2 collective-permute-done.14
  292.0 2.5 convolution_bitcast_fusion.3
  294.5 157.7 %all-reduce.16.cloned.1.call-done = f32[128,128]{0,1:T(8,128)} async-done(((f32[128,128]{0,1:T(8,128)}), f32[128,128]{0,1:T(8,128)}) %all-reduce.16.cloned.1.call-update) | async-done | bytes 65552 | tf_op jit(solution)/shard_map/psum | solution.py:66
  454.1 11.7 %cholesky.55 = f32[128,128]{1,0:T(8,128)S(1)} custom-call(f32[128,128]{1,0:T(8,128)S(1)} %fusion.94), custom_call_target="Cholesky" | custom-call | tf_op jit(solution)/shard_map/jit(cholesky)/cholesky | solution.py:67
  467.1 9.8 %custom-call.7 = f32[1,128,128]{1,2,0:T(8,128)S(1)} custom-call(f32[1,128,128]{2,1,0:T(8,128)S(1)} %fusion.90), custom_call_target="InvertDiagBlocksLowerTriangular" | custom-call | tf_op jit(solution)/shard_map/triangular_solve/custom-call.0 | solution.py:68
  478.3 1.9 collective-permute-start.16
  482.3 5.3 collective-permute-start.18
  487.5 4.3 collective-permute-done.17
  493.2 4.0 convolution_bitcast_fusion
  497.2 2.5 convolution_bitcast_fusion.1
  499.7 150.8 %all-reduce.18.cloned.1.call-done = (f32[128,128]{1,0:T(8,128)}, f32[128,128]{1,0:T(8,128)}) async-done(((f32[128,128]{1,0:T(8,128)}, f32[128,128]{1,0:T(8,128)}), (f32[128,128]{1,0:T(8,128)}, f32[128,128]{1,0:T(8,128)})) %all-reduce.18.cloned.1.call-update) | async-done | bytes 131088 | tf_op jit(solution)/shard_map/psum | solution.py:82
  (70 shorter events, 40.3 us)
Async XLA Ops:
  7.2 12.3 %copy-start = (f32[1,4,512,128]{3,2,1,0:T(8,128)S(1)}, f32[1,4,512,128]{3,2,1,0:T(8,128)}, u32[]{:S(2)}) copy-start(f32[1,4,512,128]{3,2,1,0:T(8,128)} %param.7) | copy-start | bytes 3145732
  7.2 214.3 %all-reduce.14.cloned.1.call-start = ((), (), s32[]{:S(2)}) async-start(), calls=%async_computation | async-start | bytes 131072 | tf_op jit(solution)/shard_map/psum | solution.py:66
  8.4 9.9 %collective-permute-start = (f32[1,512,128]{2,1,0:T(8,128)S(1)}, f32[1,512,128]{2,1,0:T(8,128)S(1)}, u32[]{:S(2)}, u32[]{:S(2)}) collective-permute-start(f32[1,512,128]{2,1,0:T(8,128)S(1)} %get-tuple-element.23), channel_id=1, source_target_pairs={{1,0},{2,1},{3,2},{4,3},{5,4},{6,5},{7,6},{8,7},{9,8},{10,9},{11,1... | collective-permute-start | bytes 786440 | tf_op jit(solution)/shard_map/ppermute | solution.py:18
  9.7 9.8 %collective-permute-start.1 = (f32[1,512,128]{2,1,0:T(8,128)S(1)}, f32[1,512,128]{2,1,0:T(8,128)S(1)}, u32[]{:S(2)}, u32[]{:S(2)}) collective-permute-start(f32[1,512,128]{2,1,0:T(8,128)S(1)} %get-tuple-element.24), channel_id=1, source_target_pairs={{0,1},{1,2},{2,3},{3,4},{4,5},{5,6},{6,7},{7,8},{8,9},{9,10},{10,1... | collective-permute-start | bytes 786440 | tf_op jit(solution)/shard_map/ppermute | solution.py:15
  20.7 10.7 %copy-start.2 = (f32[1,4,512]{2,1,0:T(4,128)S(1)}, f32[1,4,512]{2,1,0:T(4,128)}, u32[]{:S(2)}) copy-start(f32[1,4,512]{2,1,0:T(4,128)} %param.8) | copy-start | bytes 24580
  20.8 9.5 %collective-permute-start.2 = (f32[1,512,128]{2,1,0:T(8,128)S(1)}, f32[1,512,128]{2,1,0:T(8,128)S(1)}, u32[]{:S(2)}, u32[]{:S(2)}) collective-permute-start(f32[1,512,128]{2,1,0:T(8,128)S(1)} %get-tuple-element.21), channel_id=1, source_target_pairs={{1,0},{2,1},{3,2},{4,3},{5,4},{6,5},{7,6},{8,7},{9,8},{10,9},{11,1... | collective-permute-start | bytes 786440 | tf_op jit(solution)/shard_map/ppermute | solution.py:18
  22.1 9.4 %collective-permute-start.3 = (f32[1,512,128]{2,1,0:T(8,128)S(1)}, f32[1,512,128]{2,1,0:T(8,128)S(1)}, u32[]{:S(2)}, u32[]{:S(2)}) collective-permute-start(f32[1,512,128]{2,1,0:T(8,128)S(1)} %get-tuple-element.22), channel_id=1, source_target_pairs={{0,1},{1,2},{2,3},{3,4},{4,5},{5,6},{6,7},{7,8},{8,9},{9,10},{10,1... | collective-permute-start | bytes 786440 | tf_op jit(solution)/shard_map/ppermute | solution.py:15
  32.1 8.7 %collective-permute-start.4 = (f32[1,512,128]{2,1,0:T(8,128)S(1)}, f32[1,512,128]{2,1,0:T(8,128)S(1)}, u32[]{:S(2)}, u32[]{:S(2)}) collective-permute-start(f32[1,512,128]{2,1,0:T(8,128)S(1)} %get-tuple-element.19), channel_id=1, source_target_pairs={{1,0},{2,1},{3,2},{4,3},{5,4},{6,5},{7,6},{8,7},{9,8},{10,9},{11,1... | collective-permute-start | bytes 786440 | tf_op jit(solution)/shard_map/ppermute | solution.py:18
  33.4 8.9 %collective-permute-start.5 = (f32[1,512,128]{2,1,0:T(8,128)S(1)}, f32[1,512,128]{2,1,0:T(8,128)S(1)}, u32[]{:S(2)}, u32[]{:S(2)}) collective-permute-start(f32[1,512,128]{2,1,0:T(8,128)S(1)} %get-tuple-element.20), channel_id=1, source_target_pairs={{0,1},{1,2},{2,3},{3,4},{4,5},{5,6},{6,7},{7,8},{8,9},{9,10},{10,1... | collective-permute-start | bytes 786440 | tf_op jit(solution)/shard_map/ppermute | solution.py:15
  43.5 8.7 %collective-permute-start.6 = (f32[1,512,128]{2,1,0:T(8,128)S(1)}, f32[1,512,128]{2,1,0:T(8,128)S(1)}, u32[]{:S(2)}, u32[]{:S(2)}) collective-permute-start(f32[1,512,128]{2,1,0:T(8,128)S(1)} %get-tuple-element.17), channel_id=1, source_target_pairs={{1,0},{2,1},{3,2},{4,3},{5,4},{6,5},{7,6},{8,7},{9,8},{10,9},{11,1... | collective-permute-start | bytes 786440 | tf_op jit(solution)/shard_map/ppermute | solution.py:18
  44.8 8.9 %collective-permute-start.7 = (f32[1,512,128]{2,1,0:T(8,128)S(1)}, f32[1,512,128]{2,1,0:T(8,128)S(1)}, u32[]{:S(2)}, u32[]{:S(2)}) collective-permute-start(f32[1,512,128]{2,1,0:T(8,128)S(1)} %get-tuple-element.18), channel_id=1, source_target_pairs={{0,1},{1,2},{2,3},{3,4},{4,5},{5,6},{6,7},{7,8},{8,9},{9,10},{10,1... | collective-permute-start | bytes 786440 | tf_op jit(solution)/shard_map/ppermute | solution.py:15
  54.2 2.8 copy-start.4
  54.2 191.9 %copy-start.3 = (f32[1,2,128,128]{3,2,1,0:T(8,128)S(1)}, f32[1,2,128,128]{3,2,1,0:T(8,128)}, u32[]{:S(2)}) copy-start(f32[1,2,128,128]{3,2,1,0:T(8,128)} %param.9) | copy-start | bytes 393220
  56.8 395.5 %all-reduce.16.cloned.1.call-start = ((), (), s32[]{:S(2)}) async-start(), calls=%async_computation.1 | async-start | bytes 131072 | tf_op jit(solution)/shard_map/psum | solution.py:66
  247.6 8.3 %collective-permute-start.8 = (f32[1,512,128]{2,1,0:T(8,128)S(1)}, f32[1,512,128]{2,1,0:T(8,128)S(1)}, u32[]{:S(2)}, u32[]{:S(2)}) collective-permute-start(f32[1,512,128]{2,1,0:T(8,128)S(1)} %get-tuple-element.15), channel_id=1, source_target_pairs={{1,0},{2,1},{3,2},{4,3},{5,4},{6,5},{7,6},{8,7},{9,8},{10,9},{11,1... | collective-permute-start | bytes 786440 | tf_op jit(solution)/shard_map/ppermute | solution.py:18
  248.9 8.4 %collective-permute-start.9 = (f32[1,512,128]{2,1,0:T(8,128)S(1)}, f32[1,512,128]{2,1,0:T(8,128)S(1)}, u32[]{:S(2)}, u32[]{:S(2)}) collective-permute-start(f32[1,512,128]{2,1,0:T(8,128)S(1)} %get-tuple-element.16), channel_id=1, source_target_pairs={{0,1},{1,2},{2,3},{3,4},{4,5},{5,6},{6,7},{7,8},{8,9},{9,10},{10,1... | collective-permute-start | bytes 786440 | tf_op jit(solution)/shard_map/ppermute | solution.py:15
  257.9 8.7 %collective-permute-start.10 = (f32[1,512,128]{2,1,0:T(8,128)S(1)}, f32[1,512,128]{2,1,0:T(8,128)S(1)}, u32[]{:S(2)}, u32[]{:S(2)}) collective-permute-start(f32[1,512,128]{2,1,0:T(8,128)S(1)} %get-tuple-element.13), channel_id=1, source_target_pairs={{1,0},{2,1},{3,2},{4,3},{5,4},{6,5},{7,6},{8,7},{9,8},{10,9},{11,1... | collective-permute-start | bytes 786440 | tf_op jit(solution)/shard_map/ppermute | solution.py:18
  259.2 9.2 %collective-permute-start.11 = (f32[1,512,128]{2,1,0:T(8,128)S(1)}, f32[1,512,128]{2,1,0:T(8,128)S(1)}, u32[]{:S(2)}, u32[]{:S(2)}) collective-permute-start(f32[1,512,128]{2,1,0:T(8,128)S(1)} %get-tuple-element.14), channel_id=1, source_target_pairs={{0,1},{1,2},{2,3},{3,4},{4,5},{5,6},{6,7},{7,8},{8,9},{9,10},{10,1... | collective-permute-start | bytes 786440 | tf_op jit(solution)/shard_map/ppermute | solution.py:15
  269.0 9.1 %collective-permute-start.12 = (f32[1,512,128]{2,1,0:T(8,128)S(1)}, f32[1,512,128]{2,1,0:T(8,128)S(1)}, u32[]{:S(2)}, u32[]{:S(2)}) collective-permute-start(f32[1,512,128]{2,1,0:T(8,128)S(1)} %get-tuple-element.11), channel_id=1, source_target_pairs={{1,0},{2,1},{3,2},{4,3},{5,4},{6,5},{7,6},{8,7},{9,8},{10,9},{11,1... | collective-permute-start | bytes 786440 | tf_op jit(solution)/shard_map/ppermute | solution.py:18
  270.3 9.5 %collective-permute-start.13 = (f32[1,512,128]{2,1,0:T(8,128)S(1)}, f32[1,512,128]{2,1,0:T(8,128)S(1)}, u32[]{:S(2)}, u32[]{:S(2)}) collective-permute-start(f32[1,512,128]{2,1,0:T(8,128)S(1)} %get-tuple-element.12), channel_id=1, source_target_pairs={{0,1},{1,2},{2,3},{3,4},{4,5},{5,6},{6,7},{7,8},{8,9},{9,10},{10,1... | collective-permute-start | bytes 786440 | tf_op jit(solution)/shard_map/ppermute | solution.py:15
  281.1 8.8 %collective-permute-start.14 = (f32[1,512,128]{2,1,0:T(8,128)S(1)}, f32[1,512,128]{2,1,0:T(8,128)S(1)}, u32[]{:S(2)}, u32[]{:S(2)}) collective-permute-start(f32[1,512,128]{2,1,0:T(8,128)S(1)} %get-tuple-element.9), channel_id=1, source_target_pairs={{1,0},{2,1},{3,2},{4,3},{5,4},{6,5},{7,6},{8,7},{9,8},{10,9},{11,1... | collective-permute-start | bytes 786440 | tf_op jit(solution)/shard_map/ppermute | solution.py:18
  282.4 9.0 %collective-permute-start.15 = (f32[1,512,128]{2,1,0:T(8,128)S(1)}, f32[1,512,128]{2,1,0:T(8,128)S(1)}, u32[]{:S(2)}, u32[]{:S(2)}) collective-permute-start(f32[1,512,128]{2,1,0:T(8,128)S(1)} %get-tuple-element.10), channel_id=1, source_target_pairs={{0,1},{1,2},{2,3},{3,4},{4,5},{5,6},{6,7},{7,8},{8,9},{9,10},{10,1... | collective-permute-start | bytes 786440 | tf_op jit(solution)/shard_map/ppermute | solution.py:15
  294.5 356.0 %all-reduce.18.cloned.1.call-start = ((), (), s32[]{:S(2)}) async-start(), calls=%async_computation.2 | async-start | bytes 262144 | tf_op jit(solution)/shard_map/psum | solution.py:82
  478.3 18.9 %copy-start.1 = (f32[4,512,128]{2,1,0:T(8,128)}, f32[4,512,128]{2,1,0:T(8,128)S(1)}, u32[]{:S(2)}) copy-start(f32[4,512,128]{2,1,0:T(8,128)S(1)} %fusion.118) | copy-start | bytes 3145732
  478.3 18.9 %collective-permute-start.16 = (f32[4,512,128]{2,1,0:T(8,128)S(1)}, f32[4,512,128]{2,1,0:T(8,128)S(1)}, u32[]{:S(2)}, u32[]{:S(2)}) collective-permute-start(f32[4,512,128]{2,1,0:T(8,128)S(1)} %fusion.118), channel_id=1, source_target_pairs={{0,64},{64,128},{128,192},{192,256},{256,320},{320,384},{384,448},... | collective-permute-start | bytes 3145736 | tf_op jit(solution)/shard_map/ppermute | solution.py:26
  481.0 10.8 %collective-permute-start.17 = (f32[1,512,128]{2,1,0:T(8,128)}, f32[1,512,128]{2,1,0:T(8,128)}, u32[]{:S(2)}, u32[]{:S(2)}) collective-permute-start(f32[1,512,128]{2,1,0:T(8,128)} %get-tuple-element.7), channel_id=1, source_target_pairs={{1,0},{2,1},{3,2},{4,3},{5,4},{6,5},{7,6},{8,7},{9,8},{10,9},{11,1... | collective-permute-start | bytes 786440 | tf_op jit(solution)/shard_map/ppermute | solution.py:18
  482.3 10.9 %collective-permute-start.18 = (f32[1,512,128]{2,1,0:T(8,128)S(1)}, f32[1,512,128]{2,1,0:T(8,128)}, u32[]{:S(2)}, u32[]{:S(2)}) collective-permute-start(f32[1,512,128]{2,1,0:T(8,128)S(1)} %get-tuple-element.8), channel_id=1, source_target_pairs={{0,1},{1,2},{2,3},{3,4},{4,5},{5,6},{6,7},{7,8},{8,9},{9,10},{10,1... | collective-permute-start | bytes 786440 | tf_op jit(solution)/shard_map/ppermute | solution.py:15
Sparse Core Ops, SparseCore 0:
  56.9 164.5 all-reduce.13
  294.6 157.5 all-reduce.15
  499.8 150.6 all-reduce.17
where the time goes:
time: 659 us; the launch traced here: 658 us
  waiting for transfers between devices  512 us (78%)
  starting transfers between devices  58.7 us (9%)
  other arithmetic  56.7 us (9%)
  matrix products  14.2 us (2%)
  between operations  14.2 us (2%)
    psum x2, waiting for transfers between devices, body(): gram_sum = lax.psum(inner_modes(current, current), 'rows') / pixels  322 us
    psum x1, waiting for transfers between devices, body(): lax.psum((coupling_term, rayleigh_term), 'rows')  151 us
    ppermute x9, starting transfers between devices, padded_2(): lax.ppermute(lax.slice_in_dim(block, block.shape[dim] - width, None, axis...  44.9 us
    ppermute x9, waiting for transfers between devices, padded_2(): lax.ppermute(lax.slice_in_dim(block, 0, width, axis=dim), axis, backward)  26 us
    another operation x6, other arithmetic, body(): factor_low = jnp.linalg.cholesky(gram_sum)  24.8 us
    another operation x4, other arithmetic, body(): lax.linalg.triangular_solve(factor_low, turnings[sweep], left_side=True,...  20.9 us
  transfers between devices with their start and end apart: 22, of which 21 were waited for; matrix products, arithmetic and copies ran while one was open for 1% of the time, Pallas kernels for 0%

commit v1 on v0

--- a/solution.py
+++ b/solution.py
@@ -63,7 +63,7 @@
         for degree_step in range(2, DEGREE + 1):
             following = 2.0 * apply_edge(current, section) - before
             before, current = (current, following)
-        gram_sum = lax.psum(inner_modes(current, current), "rows") / pixels
+        gram_sum = jnp.sum(lax.all_gather(inner_modes(current, current), "rows"), axis=0) / pixels
         factor_low = jnp.linalg.cholesky(gram_sum)
         mixing = lax.linalg.triangular_solve(
             factor_low, turnings[sweep], left_side=True, lower=True, transpose_a=True

time: 659 us -> 539 us (0.82)
  waiting for transfers between devices: 512 us -> 391 us
    psum x2 -> x0, waiting for transfers between devices: 322 us -> none  [body(): gram_sum = lax.psum(inner_modes(current, current), 'rows') / pixels]
    all_gather x0 -> x2, waiting for transfers between devices: none -> 200 us  [body(): lax.all_gather(inner_modes(current, current), 'rows')]
where the time goes in v1:
time: 539 us; the launch traced here: 538 us
  waiting for transfers between devices  391 us (73%)
  starting transfers between devices  58.6 us (11%)
  other arithmetic  58.3 us (11%)
  between operations  14.2 us (3%)
  matrix products  14 us (3%)
    all_gather x2, waiting for transfers between devices, body(): lax.all_gather(inner_modes(current, current), 'rows')  200 us
    psum x1, waiting for transfers between devices, body(): lax.psum((coupling_term, rayleigh_term), 'rows')  152 us
    ppermute x9, starting transfers between devices, padded_2(): lax.ppermute(lax.slice_in_dim(block, block.shape[dim] - width, None, axis...  44.8 us
    ppermute x9, waiting for transfers between devices, padded_2(): lax.ppermute(lax.slice_in_dim(block, 0, width, axis=dim), axis, backward)  25.7 us
    another operation x6, other arithmetic, body(): factor_low = jnp.linalg.cholesky(gram_sum)  24.8 us
    another operation x4, other arithmetic, body(): lax.linalg.triangular_solve(factor_low, turnings[sweep], left_side=True,...  20.9 us
    ppermute x9, waiting for transfers between devices, padded_2(): lax.ppermute(lax.slice_in_dim(block, block.shape[dim] - width, None, axis...  12.5 us
    ppermute x9, starting transfers between devices, padded_2(): lax.ppermute(lax.slice_in_dim(block, 0, width, axis=dim), axis, backward)  11.6 us
  transfers between devices with their start and end apart: 22, of which 21 were waited for; matrix products, arithmetic and copies ran while one was open for 1% of the time, Pallas kernels for 0%

profile of v1, /device:TPU:2, one launch (start us, length us, event | category | flops | bytes accessed | tf_op | source)
XLA Modules:
  0.0 538.1 jit_solution(4606689985389857948)
XLA Ops:
  9.7 4.6 collective-permute-start.1
  14.2 4.1 collective-permute-done
  22.1 5.0 collective-permute-start.3
  27.2 3.2 collective-permute-done.2
  33.4 5.0 collective-permute-start.5
  38.4 2.4 collective-permute-done.4
  44.9 5.0 collective-permute-start.7
  49.9 2.4 collective-permute-done.6
  54.3 2.5 convolution_bitcast_fusion.5
  57.1 102.7 %all-gather.5.cloned.1.call-done = f32[8192,128]{1,0:T(8,128)} async-done(((f32[128,128]{1,0:T(8,128)}), f32[8192,128]{1,0:T(8,128)}) %all-gather.5.cloned.1.call-update) | async-done | bytes 4194320 | tf_op jit(solution)/shard_map/all_gather | solution.py:66
  159.7 2.4 reduce_sum.18
  162.4 11.7 %cholesky.44 = f32[128,128]{1,0:T(8,128)S(1)} custom-call(f32[128,128]{1,0:T(8,128)S(1)} %fusion.98), custom_call_target="Cholesky" | custom-call | tf_op jit(solution)/shard_map/jit(cholesky)/cholesky | solution.py:67
  175.4 9.8 %custom-call.6 = f32[1,128,128]{1,2,0:T(8,128)S(1)} custom-call(f32[1,128,128]{2,1,0:T(8,128)S(1)} %fusion.89), custom_call_target="InvertDiagBlocksLowerTriangular" | custom-call | tf_op jit(solution)/shard_map/triangular_solve/custom-call.0 | solution.py:68
  188.0 4.6 collective-permute-start.9
  192.6 2.4 collective-permute-done.8
  198.3 5.0 collective-permute-start.11
  203.3 2.4 collective-permute-done.10
  209.1 5.0 collective-permute-start.13
  214.1 2.4 collective-permute-done.12
  220.5 5.3 collective-permute-start.15
  225.8 2.2 collective-permute-done.14
  230.0 2.5 convolution_bitcast_fusion.3
  232.5 97.8 %all-gather.7.cloned.1.call-done = f32[8192,128]{1,0:T(8,128)} async-done(((f32[128,128]{1,0:T(8,128)}), f32[8192,128]{1,0:T(8,128)}) %all-gather.7.cloned.1.call-update) | async-done | bytes 4194320 | tf_op jit(solution)/shard_map/all_gather | solution.py:66
  330.3 2.4 reduce_sum.19
  332.9 11.7 %cholesky.55 = f32[128,128]{1,0:T(8,128)S(1)} custom-call(f32[128,128]{1,0:T(8,128)S(1)} %fusion.94), custom_call_target="Cholesky" | custom-call | tf_op jit(solution)/shard_map/jit(cholesky)/cholesky | solution.py:67
  346.0 9.8 %custom-call.7 = f32[1,128,128]{1,2,0:T(8,128)S(1)} custom-call(f32[1,128,128]{2,1,0:T(8,128)S(1)} %fusion.90), custom_call_target="InvertDiagBlocksLowerTriangular" | custom-call | tf_op jit(solution)/shard_map/triangular_solve/custom-call.0 | solution.py:68
  357.2 1.9 collective-permute-start.16
  361.1 5.3 collective-permute-start.18
  366.4 4.3 collective-permute-done.17
  372.0 3.9 convolution_bitcast_fusion
  375.9 2.5 convolution_bitcast_fusion.1
  378.4 151.9 %all-reduce.12.cloned.1.call-done = (f32[128,128]{1,0:T(8,128)}, f32[128,128]{1,0:T(8,128)}) async-done(((f32[128,128]{1,0:T(8,128)}, f32[128,128]{1,0:T(8,128)}), (f32[128,128]{1,0:T(8,128)}, f32[128,128]{1,0:T(8,128)})) %all-reduce.12.cloned.1.call-update) | async-done | bytes 131088 | tf_op jit(solution)/shard_map/psum | solution.py:82
  (74 shorter events, 40.1 us)
Async XLA Ops:
  7.2 12.3 %copy-start = (f32[1,4,512,128]{3,2,1,0:T(8,128)S(1)}, f32[1,4,512,128]{3,2,1,0:T(8,128)}, u32[]{:S(2)}) copy-start(f32[1,4,512,128]{3,2,1,0:T(8,128)} %param.7) | copy-start | bytes 3145732
  7.2 152.5 %all-gather.5.cloned.1.call-start = ((), (), s32[]{:S(2)}) async-start(), calls=%async_computation | async-start | bytes 4259840 | tf_op jit(solution)/shard_map/all_gather | solution.py:66
  8.4 9.9 %collective-permute-start = (f32[1,512,128]{2,1,0:T(8,128)S(1)}, f32[1,512,128]{2,1,0:T(8,128)S(1)}, u32[]{:S(2)}, u32[]{:S(2)}) collective-permute-start(f32[1,512,128]{2,1,0:T(8,128)S(1)} %get-tuple-element.23), channel_id=1, source_target_pairs={{1,0},{2,1},{3,2},{4,3},{5,4},{6,5},{7,6},{8,7},{9,8},{10,9},{11,1... | collective-permute-start | bytes 786440 | tf_op jit(solution)/shard_map/ppermute | solution.py:18
  9.7 9.8 %collective-permute-start.1 = (f32[1,512,128]{2,1,0:T(8,128)S(1)}, f32[1,512,128]{2,1,0:T(8,128)S(1)}, u32[]{:S(2)}, u32[]{:S(2)}) collective-permute-start(f32[1,512,128]{2,1,0:T(8,128)S(1)} %get-tuple-element.24), channel_id=1, source_target_pairs={{0,1},{1,2},{2,3},{3,4},{4,5},{5,6},{6,7},{7,8},{8,9},{9,10},{10,1... | collective-permute-start | bytes 786440 | tf_op jit(solution)/shard_map/ppermute | solution.py:15
  19.5 12.0 %copy-start.2 = (f32[1,4,512]{2,1,0:T(4,128)S(1)}, f32[1,4,512]{2,1,0:T(4,128)}, u32[]{:S(2)}) copy-start(f32[1,4,512]{2,1,0:T(4,128)} %param.8) | copy-start | bytes 24580
  20.8 9.5 %collective-permute-start.2 = (f32[1,512,128]{2,1,0:T(8,128)S(1)}, f32[1,512,128]{2,1,0:T(8,128)S(1)}, u32[]{:S(2)}, u32[]{:S(2)}) collective-permute-start(f32[1,512,128]{2,1,0:T(8,128)S(1)} %get-tuple-element.21), channel_id=1, source_target_pairs={{1,0},{2,1},{3,2},{4,3},{5,4},{6,5},{7,6},{8,7},{9,8},{10,9},{11,1... | collective-permute-start | bytes 786440 | tf_op jit(solution)/shard_map/ppermute | solution.py:18
  22.1 9.4 %collective-permute-start.3 = (f32[1,512,128]{2,1,0:T(8,128)S(1)}, f32[1,512,128]{2,1,0:T(8,128)S(1)}, u32[]{:S(2)}, u32[]{:S(2)}) collective-permute-start(f32[1,512,128]{2,1,0:T(8,128)S(1)} %get-tuple-element.22), channel_id=1, source_target_pairs={{0,1},{1,2},{2,3},{3,4},{4,5},{5,6},{6,7},{7,8},{8,9},{9,10},{10,1... | collective-permute-start | bytes 786440 | tf_op jit(solution)/shard_map/ppermute | solution.py:15
  32.1 8.7 %collective-permute-start.4 = (f32[1,512,128]{2,1,0:T(8,128)S(1)}, f32[1,512,128]{2,1,0:T(8,128)S(1)}, u32[]{:S(2)}, u32[]{:S(2)}) collective-permute-start(f32[1,512,128]{2,1,0:T(8,128)S(1)} %get-tuple-element.19), channel_id=1, source_target_pairs={{1,0},{2,1},{3,2},{4,3},{5,4},{6,5},{7,6},{8,7},{9,8},{10,9},{11,1... | collective-permute-start | bytes 786440 | tf_op jit(solution)/shard_map/ppermute | solution.py:18
  33.4 8.9 %collective-permute-start.5 = (f32[1,512,128]{2,1,0:T(8,128)S(1)}, f32[1,512,128]{2,1,0:T(8,128)S(1)}, u32[]{:S(2)}, u32[]{:S(2)}) collective-permute-start(f32[1,512,128]{2,1,0:T(8,128)S(1)} %get-tuple-element.20), channel_id=1, source_target_pairs={{0,1},{1,2},{2,3},{3,4},{4,5},{5,6},{6,7},{7,8},{8,9},{9,10},{10,1... | collective-permute-start | bytes 786440 | tf_op jit(solution)/shard_map/ppermute | solution.py:15
  43.6 8.7 %collective-permute-start.6 = (f32[1,512,128]{2,1,0:T(8,128)S(1)}, f32[1,512,128]{2,1,0:T(8,128)S(1)}, u32[]{:S(2)}, u32[]{:S(2)}) collective-permute-start(f32[1,512,128]{2,1,0:T(8,128)S(1)} %get-tuple-element.17), channel_id=1, source_target_pairs={{1,0},{2,1},{3,2},{4,3},{5,4},{6,5},{7,6},{8,7},{9,8},{10,9},{11,1... | collective-permute-start | bytes 786440 | tf_op jit(solution)/shard_map/ppermute | solution.py:18
  44.9 8.9 %collective-permute-start.7 = (f32[1,512,128]{2,1,0:T(8,128)S(1)}, f32[1,512,128]{2,1,0:T(8,128)S(1)}, u32[]{:S(2)}, u32[]{:S(2)}) collective-permute-start(f32[1,512,128]{2,1,0:T(8,128)S(1)} %get-tuple-element.18), channel_id=1, source_target_pairs={{0,1},{1,2},{2,3},{3,4},{4,5},{5,6},{6,7},{7,8},{8,9},{9,10},{10,1... | collective-permute-start | bytes 786440 | tf_op jit(solution)/shard_map/ppermute | solution.py:15
  54.3 2.7 copy-start.4
  56.8 273.5 %all-gather.7.cloned.1.call-start = ((), (), s32[]{:S(2)}) async-start(), calls=%async_computation.1 | async-start | bytes 4259840 | tf_op jit(solution)/shard_map/all_gather | solution.py:66
  159.7 25.5 %copy-start.3 = (f32[1,2,128,128]{3,2,1,0:T(8,128)S(1)}, f32[1,2,128,128]{3,2,1,0:T(8,128)}, u32[]{:S(2)}) copy-start(f32[1,2,128,128]{3,2,1,0:T(8,128)} %param.9) | copy-start | bytes 393220
  186.7 8.3 %collective-permute-start.8 = (f32[1,512,128]{2,1,0:T(8,128)S(1)}, f32[1,512,128]{2,1,0:T(8,128)S(1)}, u32[]{:S(2)}, u32[]{:S(2)}) collective-permute-start(f32[1,512,128]{2,1,0:T(8,128)S(1)} %get-tuple-element.15), channel_id=1, source_target_pairs={{1,0},{2,1},{3,2},{4,3},{5,4},{6,5},{7,6},{8,7},{9,8},{10,9},{11,1... | collective-permute-start | bytes 786440 | tf_op jit(solution)/shard_map/ppermute | solution.py:18
  188.0 8.4 %collective-permute-start.9 = (f32[1,512,128]{2,1,0:T(8,128)S(1)}, f32[1,512,128]{2,1,0:T(8,128)S(1)}, u32[]{:S(2)}, u32[]{:S(2)}) collective-permute-start(f32[1,512,128]{2,1,0:T(8,128)S(1)} %get-tuple-element.16), channel_id=1, source_target_pairs={{0,1},{1,2},{2,3},{3,4},{4,5},{5,6},{6,7},{7,8},{8,9},{9,10},{10,1... | collective-permute-start | bytes 786440 | tf_op jit(solution)/shard_map/ppermute | solution.py:15
  197.0 8.7 %collective-permute-start.10 = (f32[1,512,128]{2,1,0:T(8,128)S(1)}, f32[1,512,128]{2,1,0:T(8,128)S(1)}, u32[]{:S(2)}, u32[]{:S(2)}) collective-permute-start(f32[1,512,128]{2,1,0:T(8,128)S(1)} %get-tuple-element.13), channel_id=1, source_target_pairs={{1,0},{2,1},{3,2},{4,3},{5,4},{6,5},{7,6},{8,7},{9,8},{10,9},{11,1... | collective-permute-start | bytes 786440 | tf_op jit(solution)/shard_map/ppermute | solution.py:18
  198.3 8.9 %collective-permute-start.11 = (f32[1,512,128]{2,1,0:T(8,128)S(1)}, f32[1,512,128]{2,1,0:T(8,128)S(1)}, u32[]{:S(2)}, u32[]{:S(2)}) collective-permute-start(f32[1,512,128]{2,1,0:T(8,128)S(1)} %get-tuple-element.14), channel_id=1, source_target_pairs={{0,1},{1,2},{2,3},{3,4},{4,5},{5,6},{6,7},{7,8},{8,9},{9,10},{10,1... | collective-permute-start | bytes 786440 | tf_op jit(solution)/shard_map/ppermute | solution.py:15
  207.8 8.7 %collective-permute-start.12 = (f32[1,512,128]{2,1,0:T(8,128)S(1)}, f32[1,512,128]{2,1,0:T(8,128)S(1)}, u32[]{:S(2)}, u32[]{:S(2)}) collective-permute-start(f32[1,512,128]{2,1,0:T(8,128)S(1)} %get-tuple-element.11), channel_id=1, source_target_pairs={{1,0},{2,1},{3,2},{4,3},{5,4},{6,5},{7,6},{8,7},{9,8},{10,9},{11,1... | collective-permute-start | bytes 786440 | tf_op jit(solution)/shard_map/ppermute | solution.py:18
  209.1 8.9 %collective-permute-start.13 = (f32[1,512,128]{2,1,0:T(8,128)S(1)}, f32[1,512,128]{2,1,0:T(8,128)S(1)}, u32[]{:S(2)}, u32[]{:S(2)}) collective-permute-start(f32[1,512,128]{2,1,0:T(8,128)S(1)} %get-tuple-element.12), channel_id=1, source_target_pairs={{0,1},{1,2},{2,3},{3,4},{4,5},{5,6},{6,7},{7,8},{8,9},{9,10},{10,1... | collective-permute-start | bytes 786440 | tf_op jit(solution)/shard_map/ppermute | solution.py:15
  219.2 8.7 %collective-permute-start.14 = (f32[1,512,128]{2,1,0:T(8,128)S(1)}, f32[1,512,128]{2,1,0:T(8,128)S(1)}, u32[]{:S(2)}, u32[]{:S(2)}) collective-permute-start(f32[1,512,128]{2,1,0:T(8,128)S(1)} %get-tuple-element.9), channel_id=1, source_target_pairs={{1,0},{2,1},{3,2},{4,3},{5,4},{6,5},{7,6},{8,7},{9,8},{10,9},{11,1... | collective-permute-start | bytes 786440 | tf_op jit(solution)/shard_map/ppermute | solution.py:18
  220.5 8.9 %collective-permute-start.15 = (f32[1,512,128]{2,1,0:T(8,128)S(1)}, f32[1,512,128]{2,1,0:T(8,128)S(1)}, u32[]{:S(2)}, u32[]{:S(2)}) collective-permute-start(f32[1,512,128]{2,1,0:T(8,128)S(1)} %get-tuple-element.10), channel_id=1, source_target_pairs={{0,1},{1,2},{2,3},{3,4},{4,5},{5,6},{6,7},{7,8},{8,9},{9,10},{10,1... | collective-permute-start | bytes 786440 | tf_op jit(solution)/shard_map/ppermute | solution.py:15
  232.5 297.9 %all-reduce.12.cloned.1.call-start = ((), (), s32[]{:S(2)}) async-start(), calls=%async_computation.2 | async-start | bytes 262144 | tf_op jit(solution)/shard_map/psum | solution.py:82
  357.2 18.8 %copy-start.1 = (f32[4,512,128]{2,1,0:T(8,128)}, f32[4,512,128]{2,1,0:T(8,128)S(1)}, u32[]{:S(2)}) copy-start(f32[4,512,128]{2,1,0:T(8,128)S(1)} %fusion.118) | copy-start | bytes 3145732
  357.2 18.8 %collective-permute-start.16 = (f32[4,512,128]{2,1,0:T(8,128)S(1)}, f32[4,512,128]{2,1,0:T(8,128)S(1)}, u32[]{:S(2)}, u32[]{:S(2)}) collective-permute-start(f32[4,512,128]{2,1,0:T(8,128)S(1)} %fusion.118), channel_id=1, source_target_pairs={{0,64},{64,128},{128,192},{192,256},{256,320},{320,384},{384,448},... | collective-permute-start | bytes 3145736 | tf_op jit(solution)/shard_map/ppermute | solution.py:26
  359.8 10.8 %collective-permute-start.17 = (f32[1,512,128]{2,1,0:T(8,128)}, f32[1,512,128]{2,1,0:T(8,128)}, u32[]{:S(2)}, u32[]{:S(2)}) collective-permute-start(f32[1,512,128]{2,1,0:T(8,128)} %get-tuple-element.7), channel_id=1, source_target_pairs={{1,0},{2,1},{3,2},{4,3},{5,4},{6,5},{7,6},{8,7},{9,8},{10,9},{11,1... | collective-permute-start | bytes 786440 | tf_op jit(solution)/shard_map/ppermute | solution.py:18
  361.1 10.9 %collective-permute-start.18 = (f32[1,512,128]{2,1,0:T(8,128)S(1)}, f32[1,512,128]{2,1,0:T(8,128)}, u32[]{:S(2)}, u32[]{:S(2)}) collective-permute-start(f32[1,512,128]{2,1,0:T(8,128)S(1)} %get-tuple-element.8), channel_id=1, source_target_pairs={{0,1},{1,2},{2,3},{3,4},{4,5},{5,6},{6,7},{7,8},{8,9},{9,10},{10,1... | collective-permute-start | bytes 786440 | tf_op jit(solution)/shard_map/ppermute | solution.py:15
Sparse Core Ops, SparseCore 0:
  56.9 102.7 all-gather.4
  232.6 97.6 all-gather.6
  378.5 151.7 all-reduce.11
